TPU v7x, 32 devices: a whole 2x2x4 slice. The times are simulated.
32 devices in a mesh: dp: 8 (over z, x), tensor: 4 (over y, core).
Axes of the slice: x: 2, y: 2, z: 4, core: 2. Of those that a mesh axis runs over, the one named last changes fastest.
Arguments:
- tokens: bfloat16 [8192, 2048], P(('dp', 'tensor')), may hold values from -6 to 6
- gain_attn: float32 [2048], replicated, may hold values from 0.5 to 1.5
- gain_mlp: float32 [2048], replicated, may hold values from 0.5 to 1.5
- w_query: bfloat16 [2048, 256], P(None, 'tensor'), may hold values from -0.125 to 0.125
- w_key: bfloat16 [2048, 256], P(None, 'tensor'), may hold values from -0.125 to 0.125
- w_value: bfloat16 [2048, 2048], P(None, 'tensor'), may hold values from -0.125 to 0.125
- w_out: bfloat16 [2048, 2048], P('tensor'), may hold values from -1.5 to 1.5
- w_gate: bfloat16 [2048, 5504], P(None, 'tensor'), may hold values from -0.125 to 0.125
- w_up: bfloat16 [2048, 5504], P(None, 'tensor'), may hold values from -0.125 to 0.125
- w_down: bfloat16 [5504, 2048], P('tensor'), may hold values from -0.078125 to 0.078125
- cotangent: bfloat16 [8192, 2048], P(('dp', 'tensor')), may hold values from -6 to 6
- lengths: int32 [8], replicated, may hold values from 256 to 1024, as said below
Outputs:
- output: bfloat16 [8192, 2048], P(('dp', 'tensor'))
- input_grad: float32 [8192, 2048], P(('dp', 'tensor'))
- gain_attn_grad: float32 [2048], replicated
- gain_mlp_grad: float32 [2048], replicated
- query_grad: float32 [2048, 256], P('dp', 'tensor')
- key_grad: float32 [2048, 256], P('dp', 'tensor')
- value_grad: float32 [2048, 2048], P('dp', 'tensor')
- out_grad: float32 [2048, 2048], P('tensor', 'dp')
- gate_grad: float32 [2048, 5504], P('dp', 'tensor')
- up_grad: float32 [2048, 5504], P('dp', 'tensor')
- down_grad: float32 [5504, 2048], P('tensor', 'dp')
- den_mean: float32 [], replicated
Inputs may be any that keep to these rules, and one draw needn't show every extreme that they name: `lengths`: some sequence has length exactly 1024 and some other exactly 256.
All inputs are finite; a program needn't handle non-finite values.
Results may differ from a plain program's by a relative error of at most 0.018.
Values may be sent and summed in bfloat16 or wider, within the bound.
A program may use at most 192 MiB of HBM per device.

v0:
```python
import math

import jax
import jax.numpy as jnp
from jax import lax
from jax.sharding import PartitionSpec as P

FEAT = 16


def norm_forward(source, gain_vec):
    inv_scale = lax.rsqrt(jnp.mean(source * source, axis=-1, keepdims=True) + 1e-06)
    normal = source * inv_scale
    return (normal, inv_scale, (normal * gain_vec).astype(jnp.bfloat16))


def norm_back(grad_norm, normal, inv_scale, gain_vec):
    weighted = grad_norm * gain_vec
    return inv_scale * (weighted - normal * jnp.mean(weighted * normal, axis=-1, keepdims=True))


def per_device(
    tokens,
    gain_attn,
    gain_mlp,
    w_query,
    w_key,
    w_value,
    w_out,
    w_gate,
    w_up,
    w_down,
    cotangent,
    lengths,
):
    tok_rows = tokens.shape[0]
    groups = lax.axis_size("tensor")
    bucket = tok_rows * groups
    length = lengths[lax.axis_index("dp")]
    position = jnp.arange(bucket, dtype=jnp.int32)
    valid_rows = (position < length).astype(jnp.float32)
    own_rows = lax.axis_index("tensor") * tok_rows + jnp.arange(tok_rows, dtype=jnp.int32)
    own_valid = (own_rows < length).astype(jnp.float32)[:, None]
    head_count = w_query.shape[1] // FEAT
    head_width = w_value.shape[1] // head_count
    qk_scale = 1.0 / math.sqrt(FEAT)
    block_rows = min(512, bucket)
    float_single = jnp.float32
    bf16 = jnp.bfloat16
    x_full = tokens.astype(float_single)
    normal_attn, scale_attn, normed = norm_forward(x_full, gain_attn)
    normed_all = lax.all_gather(normed, "tensor", axis=0, tiled=True)
    query_rows = (
        jnp.dot(normed_all, w_query, preferred_element_type=float_single)
        .astype(bf16)
        .reshape(bucket, head_count, FEAT)
    )
    key_head_rows = (
        jnp.dot(normed_all, w_key, preferred_element_type=float_single)
        .astype(bf16)
        .reshape(bucket, head_count, FEAT)
    )
    value_heads = (
        jnp.dot(normed_all, w_value, preferred_element_type=float_single)
        .astype(bf16)
        .reshape(bucket, head_count, head_width)
    )

    def block_scores(first_row_index, last_row_index):
        scores = (
            jnp.einsum(
                "wra,tra->rwt",
                query_rows[first_row_index:last_row_index],
                key_head_rows[:last_row_index],
                preferred_element_type=float_single,
            )
            * qk_scale
        )
        key_mask = (
            (position[None, :last_row_index] <= position[first_row_index:last_row_index, None])
            & (position[None, :last_row_index] < length)
        ).astype(float_single)
        taylor = (1.0 + scores + 0.5 * scores * scores) * key_mask
        return (scores, key_mask, taylor)

    numer_parts = []
    denom_parts = []
    for first_row_index in range(0, bucket, block_rows):
        last_row_index = first_row_index + block_rows
        scores, key_mask, taylor = block_scores(first_row_index, last_row_index)
        numer_parts.append(
            jnp.einsum(
                "hqk,khv->qhv",
                taylor.astype(bf16),
                value_heads[:last_row_index],
                preferred_element_type=float_single,
            )
        )
        denom_parts.append(jnp.sum(taylor, axis=-1).T)
    numerator = jnp.concatenate(numer_parts, axis=0)
    denominator = jnp.concatenate(denom_parts, axis=0)
    attended = (
        (numerator / denominator[:, :, None]).reshape(bucket, head_count * head_width).astype(bf16)
    )
    den_part = jnp.sum(denominator * (valid_rows / (position + 1.0))[:, None])
    den_total = lax.psum(den_part, ("dp", "tensor"))
    attn_local = lax.psum_scatter(
        jnp.dot(attended, w_out, preferred_element_type=float_single),
        "tensor",
        scatter_dimension=0,
        tiled=True,
    )
    mid_state = x_full + attn_local
    normal_mlp, scale_mlp, normed_mlp = norm_forward(mid_state, gain_mlp)
    mlp_all = lax.all_gather(normed_mlp, "tensor", axis=0, tiled=True)
    gate_value = jnp.dot(mlp_all, w_gate, preferred_element_type=float_single)
    up_value = jnp.dot(mlp_all, w_up, preferred_element_type=float_single)
    sigmoid_gate = jax.nn.sigmoid(gate_value)
    active = gate_value * sigmoid_gate
    hidden = (active * up_value).astype(bf16)
    mlp_local = lax.psum_scatter(
        jnp.dot(hidden, w_down, preferred_element_type=float_single).astype(jnp.bfloat16),
        "tensor",
        scatter_dimension=0,
        tiled=True,
    ).astype(jnp.float32)
    output = (own_valid * (mid_state + mlp_local)).astype(bf16)
    grad_out = cotangent.astype(float_single) * own_valid
    grad_mlp_all = lax.all_gather(grad_out.astype(bf16), "tensor", axis=0, tiled=True)
    down_grad = jnp.einsum("tf,td->fd", hidden, grad_mlp_all, preferred_element_type=float_single)
    grad_hidden = jnp.einsum("td,fd->tf", grad_mlp_all, w_down, preferred_element_type=float_single)
    grad_gate = (
        grad_hidden * up_value * sigmoid_gate * (1.0 + gate_value * (1.0 - sigmoid_gate))
    ).astype(bf16)
    grad_up = (grad_hidden * active).astype(bf16)
    gate_grad = jnp.einsum("td,tf->df", mlp_all, grad_gate, preferred_element_type=float_single)
    up_grad = jnp.einsum("td,tf->df", mlp_all, grad_up, preferred_element_type=float_single)
    part_gate = jnp.einsum("tf,df->td", grad_gate, w_gate, preferred_element_type=float_single)
    part_up = jnp.einsum("tf,df->td", grad_up, w_up, preferred_element_type=float_single)
    grad_normed_mlp = lax.psum_scatter(
        part_gate + part_up, "tensor", scatter_dimension=0, tiled=True
    )
    gain_mlp_part = jnp.sum(grad_normed_mlp * normal_mlp, axis=0)
    grad_state = grad_out + norm_back(grad_normed_mlp, normal_mlp, scale_mlp, gain_mlp)
    grad_attn_all = lax.all_gather(grad_state.astype(bf16), "tensor", axis=0, tiled=True)
    out_grad = jnp.einsum("tv,td->vd", attended, grad_attn_all, preferred_element_type=float_single)
    grad_attended = jnp.einsum(
        "td,vd->tv", grad_attn_all, w_out, preferred_element_type=float_single
    ).astype(bf16)
    grad_attended = grad_attended.reshape(bucket, head_count, head_width).astype(float_single)
    grad_numerator = (grad_attended / denominator[:, :, None]).astype(bf16)
    grad_denominator = -jnp.sum(grad_attended * numerator, axis=-1) / (denominator * denominator)
    grad_value_acc = jnp.zeros((bucket, head_count, head_width), float_single)
    grad_key_acc = jnp.zeros((bucket, head_count, FEAT), float_single)
    query_parts = []
    for first_row_index in range(0, bucket, block_rows):
        last_row_index = first_row_index + block_rows
        scores, key_mask, taylor = block_scores(first_row_index, last_row_index)
        numer_block = grad_numerator[first_row_index:last_row_index]
        grad_value_acc = grad_value_acc.at[:last_row_index].add(
            jnp.einsum(
                "hqk,qhv->khv",
                taylor.astype(bf16),
                numer_block,
                preferred_element_type=float_single,
            )
        )
        taylor_feature_gradient = jnp.einsum(
            "qhv,khv->hqk",
            numer_block,
            value_heads[:last_row_index],
            preferred_element_type=float_single,
        )
        taylor_feature_gradient = (
            taylor_feature_gradient + grad_denominator[first_row_index:last_row_index].T[:, :, None]
        )
        score_gradients = (taylor_feature_gradient * key_mask * (1.0 + scores)).astype(bf16)
        query_parts.append(
            jnp.einsum(
                "dwr,rdj->wdj",
                score_gradients,
                key_head_rows[:last_row_index],
                preferred_element_type=float_single,
            )
            * qk_scale
        )
        grad_key_acc = grad_key_acc.at[:last_row_index].add(
            jnp.einsum(
                "nor,onz->rnz",
                score_gradients,
                query_rows[first_row_index:last_row_index],
                preferred_element_type=float_single,
            )
            * qk_scale
        )
    grad_queries = (
        jnp.concatenate(query_parts, axis=0).reshape(bucket, head_count * FEAT).astype(bf16)
    )
    grad_keys = grad_key_acc.reshape(bucket, head_count * FEAT).astype(bf16)
    grad_values = grad_value_acc.reshape(bucket, head_count * head_width).astype(bf16)
    query_grad = jnp.einsum(
        "td,tf->df", normed_all, grad_queries, preferred_element_type=float_single
    )
    key_grad = jnp.einsum("td,tf->df", normed_all, grad_keys, preferred_element_type=float_single)
    value_grad = jnp.einsum(
        "td,tf->df", normed_all, grad_values, preferred_element_type=float_single
    )
    part_query = jnp.einsum("tf,df->td", grad_queries, w_query, preferred_element_type=float_single)
    part_key = jnp.einsum("tf,df->td", grad_keys, w_key, preferred_element_type=float_single)
    part_value = jnp.einsum("tf,df->td", grad_values, w_value, preferred_element_type=float_single)
    grad_normed = lax.psum_scatter(
        (part_query + part_key + part_value).astype(jnp.bfloat16),
        "tensor",
        scatter_dimension=0,
        tiled=True,
    ).astype(jnp.float32)
    gain_attn_part = jnp.sum(grad_normed * normal_attn, axis=0)
    input_grad = grad_state + norm_back(grad_normed, normal_attn, scale_attn, gain_attn)
    query_total, key_total, value_total, out_total, gate_total, up_total, down_total = (
        lax.psum_scatter(
            query_grad.astype(jnp.bfloat16), "dp", scatter_dimension=0, tiled=True
        ).astype(jnp.float32),
        lax.psum_scatter(
            key_grad.astype(jnp.bfloat16), "dp", scatter_dimension=0, tiled=True
        ).astype(jnp.float32),
        lax.psum_scatter(
            value_grad.astype(jnp.bfloat16), "dp", scatter_dimension=0, tiled=True
        ).astype(jnp.float32),
        lax.psum_scatter(
            out_grad.astype(jnp.bfloat16), "dp", scatter_dimension=1, tiled=True
        ).astype(jnp.float32),
        lax.psum_scatter(
            gate_grad.astype(jnp.bfloat16), "dp", scatter_dimension=0, tiled=True
        ).astype(jnp.float32),
        lax.psum_scatter(
            up_grad.astype(jnp.bfloat16), "dp", scatter_dimension=0, tiled=True
        ).astype(jnp.float32),
        lax.psum_scatter(
            down_grad.astype(jnp.bfloat16), "dp", scatter_dimension=1, tiled=True
        ).astype(jnp.float32),
    )
    gain_attn_total, gain_mlp_total = lax.psum((gain_attn_part, gain_mlp_part), ("dp", "tensor"))
    den_mean = den_total / (head_count * groups * jnp.sum(lengths).astype(float_single))
    return (
        output,
        input_grad,
        gain_attn_total,
        gain_mlp_total,
        query_total,
        key_total,
        value_total,
        out_total,
        gate_total,
        up_total,
        down_total,
        den_mean,
    )


def solution(mesh):
    return jax.shard_map(
        per_device,
        mesh=mesh,
        in_specs=(
            P(("dp", "tensor"), None),
            P(),
            P(),
            P(None, "tensor"),
            P(None, "tensor"),
            P(None, "tensor"),
            P("tensor", None),
            P(None, "tensor"),
            P(None, "tensor"),
            P("tensor", None),
            P(("dp", "tensor"), None),
            P(),
        ),
        out_specs=(
            P(("dp", "tensor"), None),
            P(("dp", "tensor"), None),
            P(),
            P(),
            P("dp", "tensor"),
            P("dp", "tensor"),
            P("dp", "tensor"),
            P("tensor", "dp"),
            P("dp", "tensor"),
            P("dp", "tensor"),
            P("tensor", "dp"),
            P(),
        ),
        check_vma=False,
    )
```

profile of v0, /device:TPU:0, one launch (start us, length us, event | category | flops | bytes accessed | tf_op | source)
XLA Modules:
  0.0 1130.0 jit_solution(7455526323109062894)
XLA Ops:
  16.0 33.4 %all-gather.5.cloned.1.call-done = bf16[1024,2048]{1,0:T(8,128)(2,1)} async-done(((bf16[256,2048]{1,0:T(8,128)(2,1)}), bf16[1024,2048]{1,0:T(8,128)(2,1)}) %all-gather.5.cloned.1.call-update) | async-done | bytes 4194320 | tf_op jit(solution)/shard_map/all_gather | solution.py:52
  59.3 4.7 fusion.1
  69.2 5.6 fusion.41
  74.9 71.8 %reduce-scatter.12.cloned.1.call-done = f32[256,2048]{1,0:T(8,128)} async-done(((f32[1024,2048]{1,0:T(8,128)}), f32[256,2048]{1,0:T(8,128)}) %reduce-scatter.12.cloned.1.call-update) | async-done | bytes 2097168 | tf_op jit(solution)/shard_map/reduce_scatter | solution.py:107
  153.4 32.4 %all-gather.7.cloned.1.call-done = bf16[1024,2048]{1,0:T(8,128)(2,1)} async-done(((bf16[256,2048]{1,0:T(8,128)(2,1)}), bf16[1024,2048]{1,0:T(8,128)(2,1)}) %all-gather.7.cloned.1.call-update) | async-done | bytes 4194320 | tf_op jit(solution)/shard_map/all_gather | solution.py:115
  185.9 11.4 %fusion.42 = f32[1024,1376]{0,1:T(8,128)} fusion(bf16[1024,2048]{1,0:T(8,128)(2,1)} %all-gather.7.cloned.1.call-done, bf16[2048,1376]{0,1:T(8,128)(2,1)} %param.31), kind=kOutput, calls=%fused_computation.98 | convolution fusion | flops 5771362304 | bytes 15466496 | tf_op jit(solution)/shard_map/dot_general | solution.py:116
  197.3 9.6 fusion.43
  206.9 15.5 %all-gather.9.cloned.1.call-done = bf16[1024,2048]{1,0:T(8,128)(2,1)} async-done(((bf16[256,2048]{1,0:T(8,128)(2,1)}), bf16[1024,2048]{1,0:T(8,128)(2,1)}) %all-gather.9.cloned.1.call-update) | async-done | bytes 4194320 | tf_op jit(solution)/shard_map/all_gather | solution.py:129
  222.4 14.8 %multiply_convert_fusion.1 = (bf16[1024,1376]{0,1:T(8,128)(2,1)S(1)}, bf16[1024,1376]{0,1:T(8,128)(2,1)S(1)}, bf16[1024,1376]{0,1:T(8,128)(2,1)}) fusion(f32[1024,1376]{0,1:T(8,128)} %fusion.42, f32[1024,1376]{0,1:T(8,128)} %fusion.43, bf16[1024,2048]{1,0:T(8,128)(2,1)} %all-gather.9.cloned.1.call-done, bf16[1376,2048]{1,0:T(8,128)(2,1)} %param.33), kind=kOutput, calls=%fused_computation.6 | convolution fusion | flops 5792497664 | bytes 29556736 | tf_op jit(solution)/shard_map/td,fd->tf/dot_general | solution.py:131
  237.2 11.0 fusion.44
  248.3 11.6 %convolution_add_fusion = f32[1024,2048]{1,0:T(8,128)} fusion(f32[1024,2048]{1,0:T(8,128)S(1)} %fusion.44, bf16[1024,1376]{0,1:T(8,128)(2,1)S(1)} %get-tuple-element.87, bf16[2048,1376]{0,1:T(8,128)(2,1)} %param.32), kind=kOutput, calls=%fused_computation.15 | convolution fusion | flops 5773459456 | bytes 25231360 | tf_op jit(solution)/shard_map/tf,df->td/dot_general | solution.py:139
  259.9 11.1 convolution_convert_fusion.3
  271.1 60.7 %reduce-scatter.16.cloned.1.call-done = f32[256,2048]{1,0:T(8,128)} async-done(((f32[1024,2048]{1,0:T(8,128)}), f32[256,2048]{1,0:T(8,128)}) %reduce-scatter.16.cloned.1.call-update) | async-done | bytes 2097168 | tf_op jit(solution)/shard_map/reduce_scatter | solution.py:140
  334.6 44.1 %reduce-scatter.14.cloned.1.call-done = bf16[256,2048]{1,0:T(8,128)(2,1)} async-done(((bf16[1024,2048]{1,0:T(8,128)(2,1)}), bf16[256,2048]{1,0:T(8,128)(2,1)}) %reduce-scatter.14.cloned.1.call-update) | async-done | bytes 1048592 | tf_op jit(solution)/shard_map/reduce_scatter | solution.py:121
  378.7 5.4 fusion.38
  384.2 10.2 convolution_convert_fusion.1
  394.5 10.4 convolution_convert_fusion
  404.9 10.2 convolution_convert_fusion.2
  418.8 5.0 fusion.13
  427.1 5.1 multiply_convert_fusion
  443.3 6.3 convolution_convert_fusion.4
  449.6 3.9 convolution_bitcast_fusion
  456.2 3.8 convolution_convert_fusion.5
  470.4 61.0 %reduce-scatter.28.cloned.1.call-done = bf16[256,1376]{0,1:T(8,128)(2,1)} async-done(((bf16[2048,1376]{0,1:T(8,128)(2,1)}), bf16[256,1376]{0,1:T(8,128)(2,1)}) %reduce-scatter.28.cloned.1.call-update) | async-done | bytes 704528 | tf_op jit(solution)/shard_map/reduce_scatter | solution.py:232
  533.7 110.1 %reduce-scatter.30.cloned.1.call-done = bf16[256,1376]{0,1:T(8,128)(2,1)} async-done(((bf16[2048,1376]{0,1:T(8,128)(2,1)}), bf16[256,1376]{0,1:T(8,128)(2,1)}) %reduce-scatter.30.cloned.1.call-update) | async-done | bytes 704528 | tf_op jit(solution)/shard_map/reduce_scatter | solution.py:235
  646.1 109.9 %reduce-scatter.32.cloned.1.call-done = bf16[1376,256]{1,0:T(8,128)(2,1)} async-done(((bf16[1376,2048]{1,0:T(8,128)(2,1)}), bf16[1376,256]{1,0:T(8,128)(2,1)}) %reduce-scatter.32.cloned.1.call-update) | async-done | bytes 704528 | tf_op jit(solution)/shard_map/reduce_scatter | solution.py:238
  758.3 63.4 %reduce-scatter.22.cloned.1.call-done = bf16[256,64]{0,1:T(8,128)(2,1)} async-done(((bf16[2048,64]{0,1:T(8,128)(2,1)}), bf16[256,64]{0,1:T(8,128)(2,1)}) %reduce-scatter.22.cloned.1.call-update) | async-done | bytes 32784 | tf_op jit(solution)/shard_map/reduce_scatter | solution.py:223
  823.1 63.5 %reduce-scatter.20.cloned.1.call-done = bf16[256,64]{0,1:T(8,128)(2,1)} async-done(((bf16[2048,64]{0,1:T(8,128)(2,1)}), bf16[256,64]{0,1:T(8,128)(2,1)}) %reduce-scatter.20.cloned.1.call-update) | async-done | bytes 32784 | tf_op jit(solution)/shard_map/reduce_scatter | solution.py:220
  888.0 70.0 %reduce-scatter.26.cloned.1.call-done = bf16[512,256]{1,0:T(8,128)(2,1)} async-done(((bf16[512,2048]{1,0:T(8,128)(2,1)}), bf16[512,256]{1,0:T(8,128)(2,1)}) %reduce-scatter.26.cloned.1.call-update) | async-done | bytes 262160 | tf_op jit(solution)/shard_map/reduce_scatter | solution.py:229
  959.8 69.6 %reduce-scatter.24.cloned.1.call-done = bf16[256,512]{1,0:T(8,128)(2,1)} async-done(((bf16[2048,512]{1,0:T(8,128)(2,1)}), bf16[256,512]{1,0:T(8,128)(2,1)}) %reduce-scatter.24.cloned.1.call-update) | async-done | bytes 262160 | tf_op jit(solution)/shard_map/reduce_scatter | solution.py:226
  1031.2 44.3 %reduce-scatter.18.cloned.1.call-done = bf16[256,2048]{1,0:T(8,128)(2,1)} async-done(((bf16[1024,2048]{1,0:T(8,128)(2,1)}), bf16[256,2048]{1,0:T(8,128)(2,1)}) %reduce-scatter.18.cloned.1.call-update) | async-done | bytes 1048592 | tf_op jit(solution)/shard_map/reduce_scatter | solution.py:211
  1077.6 39.9 %all-reduce.2 = (f32[2048]{0:T(1024)}, f32[2048]{0:T(1024)}, f32[]{:T(128)}) all-reduce(f32[2048]{0:T(1024)S(1)} %get-tuple-element.78, f32[2048]{0:T(1024)S(1)} %get-tuple-element.76, f32[]{:T(128)} %get-tuple-element.95), channel_id=1, replica_groups=mesh['dp'=8,'tensor'=4] {'dp','tensor'}, use_global_device_ids=true, to_apply=%region_12.0 | all-reduce | flops 4097 | bytes 32776 | tf_op jit(solution)/shard_map/psum | solution.py:242
  (170 shorter events, 82.6 us)
Async XLA Ops:
  7.2 62.0 %copy-start = (bf16[512,2048]{1,0:T(8,128)(2,1)S(1)}, bf16[512,2048]{1,0:T(8,128)(2,1)}, u32[]{:S(2)}) copy-start(bf16[512,2048]{1,0:T(8,128)(2,1)} %param.30) | copy-start | bytes 6291460
  7.2 42.2 %copy-start.28 = (bf16[2048,64]{0,1:T(8,128)(2,1)S(1)}, bf16[2048,64]{0,1:T(8,128)(2,1)}, u32[]{:S(2)}) copy-start(bf16[2048,64]{0,1:T(8,128)(2,1)} %param.27) | copy-start | bytes 786436
  7.2 42.1 %all-gather.5.cloned.1.call-start = ((), (), s32[]{:S(2)}) async-start(), calls=%async_computation.11 | async-start | bytes 5242880 | tf_op jit(solution)/shard_map/all_gather | solution.py:52
  12.0 134.7 %reduce-scatter.12.cloned.1.call-start = ((), (), s32[]{:S(2)}) async-start(), calls=%async_computation.12 | async-start | bytes 10485760 | tf_op jit(solution)/shard_map/reduce_scatter | solution.py:107
  14.3 49.8 %copy-start.16 = (f32[512,512]{0,1:T(8,128)}, f32[512,512]{0,1:T(8,128)S(1)}, u32[]{:S(2)}) copy-start(f32[512,512]{0,1:T(8,128)S(1)} %and_convert_fusion) | copy-start | bytes 3145732
  57.1 8.2 copy-start.12
  57.2 6.9 copy-start.24
  58.5 5.6 copy-start.14
  74.8 71.9 %copy-start.7 = (bf16[256,2048]{1,0:T(8,128)(2,1)S(1)}, bf16[256,2048]{1,0:T(8,128)(2,1)}, u32[]{:S(2)}) copy-start(bf16[256,2048]{1,0:T(8,128)(2,1)} %param.24) | copy-start | bytes 3145732
  74.8 75.1 %copy-start.32 = (f32[2048]{0:T(1024)S(1)}, f32[2048]{0:T(1024)}, u32[]{:S(2)}) copy-start(f32[2048]{0:T(1024)} %param.26) | copy-start | bytes 24580
  74.9 111.0 %all-gather.7.cloned.1.call-start = ((), (), s32[]{:S(2)}) async-start(), calls=%async_computation.13 | async-start | bytes 5242880 | tf_op jit(solution)/shard_map/all_gather | solution.py:115
  151.2 71.2 %all-gather.9.cloned.1.call-start = ((), (), s32[]{:S(2)}) async-start(), calls=%async_computation.15 | async-start | bytes 5242880 | tf_op jit(solution)/shard_map/all_gather | solution.py:129
  153.2 178.6 %reduce-scatter.16.cloned.1.call-start = ((), (), s32[]{:S(2)}) async-start(), calls=%async_computation.16 | async-start | bytes 10485760 | tf_op jit(solution)/shard_map/reduce_scatter | solution.py:140
  185.9 11.4 %copy-start.35 = (bf16[1024,2048]{1,0:T(8,128)(2,1)S(1)}, bf16[1024,2048]{1,0:T(8,128)(2,1)}, u32[]{:S(2)}) copy-start(bf16[1024,2048]{1,0:T(8,128)(2,1)} %all-gather.7.cloned.1.call-done) | copy-start | bytes 12582916
  237.2 11.0 copy-start.40
  237.2 11.0 copy-start.21
  259.9 118.8 %reduce-scatter.14.cloned.1.call-start = ((), (), s32[]{:S(2)}) async-start(), calls=%async_computation.14 | async-start | bytes 5242880 | tf_op jit(solution)/shard_map/reduce_scatter | solution.py:121
  271.0 147.7 %all-gather.11.cloned.1.call-start = ((), (), s32[]{:S(2)}) async-start(), calls=%async_computation.17 | async-start | bytes 5242880 | tf_op jit(solution)/shard_map/all_gather | solution.py:145
  384.1 147.3 %reduce-scatter.28.cloned.1.call-start = ((), (), s32[]{:S(2)}) async-start(), calls=%async_computation.23 | async-start | bytes 6340608 | tf_op jit(solution)/shard_map/reduce_scatter | solution.py:232
  394.4 249.3 %reduce-scatter.30.cloned.1.call-start = ((), (), s32[]{:S(2)}) async-start(), calls=%async_computation.24 | async-start | bytes 6340608 | tf_op jit(solution)/shard_map/reduce_scatter | solution.py:235
  404.9 351.1 %reduce-scatter.32.cloned.1.call-start = ((), (), s32[]{:S(2)}) async-start(), calls=%async_computation.25 | async-start | bytes 6340608 | tf_op jit(solution)/shard_map/reduce_scatter | solution.py:238
  415.2 406.5 %reduce-scatter.22.cloned.1.call-start = ((), (), s32[]{:S(2)}) async-start(), calls=%async_computation.20 | async-start | bytes 294912 | tf_op jit(solution)/shard_map/reduce_scatter | solution.py:223
  418.8 5.9 copy-start.15
  418.8 5.9 copy-start.17
  418.8 5.9 copy-start.25
  437.1 449.5 %reduce-scatter.20.cloned.1.call-start = ((), (), s32[]{:S(2)}) async-start(), calls=%async_computation.19 | async-start | bytes 294912 | tf_op jit(solution)/shard_map/reduce_scatter | solution.py:220
  443.2 514.8 %reduce-scatter.26.cloned.1.call-start = ((), (), s32[]{:S(2)}) async-start(), calls=%async_computation.22 | async-start | bytes 2359296 | tf_op jit(solution)/shard_map/reduce_scatter | solution.py:229
  449.6 579.9 %reduce-scatter.24.cloned.1.call-start = ((), (), s32[]{:S(2)}) async-start(), calls=%async_computation.21 | async-start | bytes 2359296 | tf_op jit(solution)/shard_map/reduce_scatter | solution.py:226
  460.0 615.5 %reduce-scatter.18.cloned.1.call-start = ((), (), s32[]{:S(2)}) async-start(), calls=%async_computation.18 | async-start | bytes 5242880 | tf_op jit(solution)/shard_map/reduce_scatter | solution.py:211
  469.1 606.4 %copy-start.8 = (bf16[256,2048]{1,0:T(8,128)(2,1)S(1)}, bf16[256,2048]{1,0:T(8,128)(2,1)}, u32[]{:S(2)}) copy-start(bf16[256,2048]{1,0:T(8,128)(2,1)} %param.24) | copy-start | bytes 3145732
  469.1 606.4 %copy-start.31 = (f32[2048]{0:T(1024)S(1)}, f32[2048]{0:T(1024)}, u32[]{:S(2)}) copy-start(f32[2048]{0:T(1024)} %param.25) | copy-start | bytes 24580
  469.1 606.4 %copy-start.34 = (f32[256]{0:T(256)S(1)}, f32[256]{0:T(256)}, u32[]{:S(2)}) copy-start(f32[256]{0:T(256)} %copy-done.33) | copy-start | bytes 3076
  (24 other events, 56.6 us)
Sparse Core Ops, SparseCore 0:
  12.1 37.1 all-gather.4
  75.0 71.7 reduce-scatter.11
  151.3 34.4 all-gather.6
  187.9 34.4 all-gather.8
  260.0 71.6 reduce-scatter.15
  334.1 44.5 reduce-scatter.13
  384.2 34.4 all-gather.10
  422.9 108.4 reduce-scatter.27
  535.5 108.2 reduce-scatter.29
  647.7 108.2 reduce-scatter.31
  760.3 61.4 reduce-scatter.21
  825.8 60.7 reduce-scatter.19
  890.5 67.4 reduce-scatter.25
  962.4 66.9 reduce-scatter.23
  1031.9 43.5 reduce-scatter.17
where the time goes:
time: 1140 us; the launch traced here: 1130 us
  waiting for transfers between devices  853 us (75%)
  matrix products  166 us (15%)
  other arithmetic  42.2 us (4%)
  blocking collectives  39.9 us (4%)
  between operations  17.4 us (2%)
    reduce_scatter x1, waiting for transfers between devices, per_device(): lax.psum_scatter(up_grad.astype(jnp.bfloat16), 'dp', scatter_dimension=0,...  110 us
    reduce_scatter x1, waiting for transfers between devices, per_device(): lax.psum_scatter(down_grad.astype(jnp.bfloat16), 'dp', scatter_dimension=...  110 us
    reduce_scatter x1, waiting for transfers between devices, per_device(): lax.psum_scatter(jnp.dot(attended, w_out, preferred_element_type=float_si...  71.8 us
    reduce_scatter x1, waiting for transfers between devices, per_device(): lax.psum_scatter(out_grad.astype(jnp.bfloat16), 'dp', scatter_dimension=1...  70 us
    reduce_scatter x1, waiting for transfers between devices, per_device(): lax.psum_scatter(value_grad.astype(jnp.bfloat16), 'dp', scatter_dimension...  69.6 us
    reduce_scatter x1, waiting for transfers between devices, per_device(): lax.psum_scatter(query_grad.astype(jnp.bfloat16), 'dp', scatter_dimension...  63.5 us
    reduce_scatter x1, waiting for transfers between devices, per_device(): lax.psum_scatter(key_grad.astype(jnp.bfloat16), 'dp', scatter_dimension=0...  63.4 us
    reduce_scatter x1, waiting for transfers between devices, per_device(): lax.psum_scatter(gate_grad.astype(jnp.bfloat16), 'dp', scatter_dimension=...  61 us
  transfers between devices with their start and end apart: 15, of which 15 were waited for; matrix products, arithmetic and copies ran while one was open for 12% of the time, Pallas kernels for 0%

commit v1 on v0

--- a/solution.py
+++ b/solution.py
@@ -1,11 +1,142 @@
+import functools
 import math
 
 import jax
 import jax.numpy as jnp
 from jax import lax
+from jax.experimental import pallas as pl
+from jax.experimental.pallas import tpu as pltpu
 from jax.sharding import PartitionSpec as P
 
 FEAT = 16
+MESH = pl.DeviceIdType.MESH
+f32 = jnp.float32
+bf16 = jnp.bfloat16
+
+
+def weight_kernel(dp_size, count, x_of, *refs):
+    n_x = max(x_of) + 1
+    lefts, refs = refs[:n_x], refs[n_x:]
+    rights, refs = refs[:count], refs[count:]
+    outs, refs = refs[:count], refs[count:]
+    xsend, xrecv, zsend, zrecv = (refs[i * count : (i + 1) * count] for i in range(4))
+    xs_sem, xr_sem, zs_sem, zr_sem = refs[4 * count :]
+    nz = dp_size // 2
+    rows = outs[0].shape[0]
+    dp = lax.axis_index("dp")
+    tensor = lax.axis_index("tensor")
+    z, x = dp // 2, lax.rem(dp, 2)
+    partner = (z * 2 + 1 - x, tensor)
+
+    def target(k):
+        return lax.rem(z + 1 + k, nz)
+
+    barrier = pltpu.get_barrier_semaphore()
+    pl.semaphore_signal(barrier, inc=1, device_id=partner, device_id_type=MESH)
+    for k in range(nz - 1):
+        pl.semaphore_signal(barrier, inc=1, device_id=(target(k) * 2 + x, tensor), device_id_type=MESH)
+    pl.semaphore_wait(barrier, nz)
+
+    def block(i, zt, xt):
+        start = pl.multiple_of((zt * 2 + xt) * rows, rows)
+        if rows % 128:
+            left, dims = lefts[x_of[i]][pl.ds(start, rows), :], ((1,), (0,))
+        else:
+            left, dims = lefts[x_of[i]][:, pl.ds(start, rows)], ((0,), (0,))
+        return lax.dot_general(left, rights[i][...], (dims, ((), ())), preferred_element_type=f32)
+
+    def xcopy(i, k):
+        return pltpu.make_async_remote_copy(
+            xsend[i].at[k], xrecv[i].at[k], xs_sem.at[i, k], xr_sem.at[i, k], device_id=partner, device_id_type=MESH
+        )
+
+    def zcopy(i, k):
+        return pltpu.make_async_remote_copy(
+            zsend[i].at[k], zrecv[i].at[k], zs_sem.at[i, k], zr_sem.at[i, k],
+            device_id=(target(k) * 2 + x, tensor), device_id_type=MESH,
+        )
+
+    def cross(i):
+        def body(k, carry):
+            xsend[i][k] = block(i, target(k), 1 - x).astype(bf16)
+            if i == 0:
+                @pl.when(k < 2)
+                def _():
+                    xcopy(i, k).start()
+            return carry
+        lax.fori_loop(0, nz, body, 0)
+
+    def more(i, k):
+        if i + 1 < count:
+            later = k + 2
+            @pl.when(later < nz)
+            def _():
+                xcopy(i, later).start()
+            @pl.when(later >= nz)
+            def _():
+                xcopy(i + 1, later - nz).start()
+        else:
+            @pl.when(k + 2 < nz)
+            def _():
+                xcopy(i, k + 2).start()
+
+    def keep(i):
+        def body(k, carry):
+            own = block(i, target(k), x)
+            xcopy(i, k).wait_recv()
+            more(i, k)
+            zsend[i][k] = (own + xrecv[i][k].astype(f32)).astype(bf16)
+            zcopy(i, k).start()
+            return carry
+        lax.fori_loop(0, nz - 1, body, 0)
+        own = block(i, z, x)
+        xcopy(i, nz - 1).wait_recv()
+        more(i, nz - 1)
+        outs[i][...] = own + xrecv[i][nz - 1].astype(f32)
+
+    cross(0)
+    for i in range(count):
+        if i + 1 < count:
+            cross(i + 1)
+        keep(i)
+    for i in range(count):
+        def add(k, carry):
+            zcopy(i, k).wait_recv()
+            outs[i][...] += zrecv[i][k].astype(f32)
+            return carry
+        lax.fori_loop(0, nz - 1, add, 0)
+    for i in range(count):
+        def done(k, carry):
+            zcopy(i, k).wait_send()
+            return carry
+        lax.fori_loop(0, nz - 1, done, 0)
+        def donex(k, carry):
+            xcopy(i, k).wait_send()
+            return carry
+        lax.fori_loop(0, nz, donex, 0)
+
+
+def weight_sums(lefts, rights, x_of, collective_id):
+    dp_size = lax.axis_size("dp")
+    nz = dp_size // 2
+    count = len(rights)
+    rows = lefts[0].shape[1] // dp_size
+    if rows % 128:
+        lefts = [left.T for left in lefts]
+    buf = lambda n: [pltpu.VMEM((n, rows, r.shape[1]), bf16) for r in rights]
+    vm = pl.BlockSpec(memory_space=pltpu.VMEM)
+    sem = lambda n: pltpu.SemaphoreType.DMA((count, n))
+    return pl.pallas_call(
+        functools.partial(weight_kernel, dp_size, count, x_of),
+        out_shape=[jax.ShapeDtypeStruct((rows, r.shape[1]), f32) for r in rights],
+        in_specs=[vm] * (len(lefts) + count),
+        out_specs=[vm] * count,
+        scratch_shapes=buf(nz) + buf(nz) + buf(nz - 1) + buf(nz - 1) + [sem(nz), sem(nz), sem(nz - 1), sem(nz - 1)],
+        compiler_params=pltpu.CompilerParams(
+            collective_id=collective_id, has_side_effects=True, vmem_limit_bytes=60 << 20
+        ),
+        name="weight_sums",
+    )(*lefts, *rights)
 
 
 def norm_forward(source, gain_vec):
@@ -127,14 +258,11 @@
     output = (own_valid * (mid_state + mlp_local)).astype(bf16)
     grad_out = cotangent.astype(float_single) * own_valid
     grad_mlp_all = lax.all_gather(grad_out.astype(bf16), "tensor", axis=0, tiled=True)
-    down_grad = jnp.einsum("tf,td->fd", hidden, grad_mlp_all, preferred_element_type=float_single)
     grad_hidden = jnp.einsum("td,fd->tf", grad_mlp_all, w_down, preferred_element_type=float_single)
     grad_gate = (
         grad_hidden * up_value * sigmoid_gate * (1.0 + gate_value * (1.0 - sigmoid_gate))
     ).astype(bf16)
     grad_up = (grad_hidden * active).astype(bf16)
-    gate_grad = jnp.einsum("td,tf->df", mlp_all, grad_gate, preferred_element_type=float_single)
-    up_grad = jnp.einsum("td,tf->df", mlp_all, grad_up, preferred_element_type=float_single)
     part_gate = jnp.einsum("tf,df->td", grad_gate, w_gate, preferred_element_type=float_single)
     part_up = jnp.einsum("tf,df->td", grad_up, w_up, preferred_element_type=float_single)
     grad_normed_mlp = lax.psum_scatter(
@@ -143,7 +271,6 @@
     gain_mlp_part = jnp.sum(grad_normed_mlp * normal_mlp, axis=0)
     grad_state = grad_out + norm_back(grad_normed_mlp, normal_mlp, scale_mlp, gain_mlp)
     grad_attn_all = lax.all_gather(grad_state.astype(bf16), "tensor", axis=0, tiled=True)
-    out_grad = jnp.einsum("tv,td->vd", attended, grad_attn_all, preferred_element_type=float_single)
     grad_attended = jnp.einsum(
         "td,vd->tv", grad_attn_all, w_out, preferred_element_type=float_single
     ).astype(bf16)
@@ -198,13 +325,6 @@
     )
     grad_keys = grad_key_acc.reshape(bucket, head_count * FEAT).astype(bf16)
     grad_values = grad_value_acc.reshape(bucket, head_count * head_width).astype(bf16)
-    query_grad = jnp.einsum(
-        "td,tf->df", normed_all, grad_queries, preferred_element_type=float_single
-    )
-    key_grad = jnp.einsum("td,tf->df", normed_all, grad_keys, preferred_element_type=float_single)
-    value_grad = jnp.einsum(
-        "td,tf->df", normed_all, grad_values, preferred_element_type=float_single
-    )
     part_query = jnp.einsum("tf,df->td", grad_queries, w_query, preferred_element_type=float_single)
     part_key = jnp.einsum("tf,df->td", grad_keys, w_key, preferred_element_type=float_single)
     part_value = jnp.einsum("tf,df->td", grad_values, w_value, preferred_element_type=float_single)
@@ -216,29 +336,20 @@
     ).astype(jnp.float32)
     gain_attn_part = jnp.sum(grad_normed * normal_attn, axis=0)
     input_grad = grad_state + norm_back(grad_normed, normal_attn, scale_attn, gain_attn)
-    query_total, key_total, value_total, out_total, gate_total, up_total, down_total = (
-        lax.psum_scatter(
-            query_grad.astype(jnp.bfloat16), "dp", scatter_dimension=0, tiled=True
-        ).astype(jnp.float32),
-        lax.psum_scatter(
-            key_grad.astype(jnp.bfloat16), "dp", scatter_dimension=0, tiled=True
-        ).astype(jnp.float32),
-        lax.psum_scatter(
-            value_grad.astype(jnp.bfloat16), "dp", scatter_dimension=0, tiled=True
-        ).astype(jnp.float32),
-        lax.psum_scatter(
-            out_grad.astype(jnp.bfloat16), "dp", scatter_dimension=1, tiled=True
-        ).astype(jnp.float32),
-        lax.psum_scatter(
-            gate_grad.astype(jnp.bfloat16), "dp", scatter_dimension=0, tiled=True
-        ).astype(jnp.float32),
-        lax.psum_scatter(
-            up_grad.astype(jnp.bfloat16), "dp", scatter_dimension=0, tiled=True
-        ).astype(jnp.float32),
-        lax.psum_scatter(
-            down_grad.astype(jnp.bfloat16), "dp", scatter_dimension=1, tiled=True
-        ).astype(jnp.float32),
-    )
+    down_total, gate_total, up_total = weight_sums(
+        (grad_mlp_all, mlp_all), (hidden, grad_gate, grad_up), (0, 1, 1), 1
+    )
+    qk_width = head_count * FEAT
+    out_total, qkv_total = weight_sums(
+        (grad_attn_all, normed_all),
+        (attended, jnp.concatenate([grad_values, grad_queries, grad_keys], axis=1)),
+        (0, 1),
+        2,
+    )
+    value_width = head_count * head_width
+    value_total = qkv_total[:, :value_width]
+    query_total = qkv_total[:, value_width : value_width + qk_width]
+    key_total = qkv_total[:, value_width + qk_width :]
     gain_attn_total, gain_mlp_total = lax.psum((gain_attn_part, gain_mlp_part), ("dp", "tensor"))
     den_mean = den_total / (head_count * groups * jnp.sum(lengths).astype(float_single))
     return (
@@ -249,10 +360,10 @@
         query_total,
         key_total,
         value_total,
-        out_total,
+        out_total.T,
         gate_total,
         up_total,
-        down_total,
+        down_total.T,
         den_mean,
     )
 

time: 1140 us -> 832 us (0.73)
  waiting for transfers between devices: 853 us -> 289 us
  Pallas kernels: 0 us -> 285 us
  matrix products: 166 us -> 124 us
  local copies, waits for them, and re-layouts: 10.3 us -> 34.7 us
    reduce_scatter x7 -> x0, waiting for transfers between devices: 548 us -> none  [the longest x1 110 us: per_device(): lax.psum_scatter(up_grad.astype(jnp.bfloat16), 'dp', scatter_dimension=0,...]
    pallas_call x0 -> x2, Pallas kernels: none -> 285 us  [weight_sums(): pl.pallas_call(functools.partial(weight_kernel, dp_size, count, x_of), ou...]
    dot_general x7 -> x0, matrix products: 46.3 us -> none  [the longest x1 10.4 us: per_device(): jnp.einsum('td,tf->df', mlp_all, grad_up, preferred_element_type=float_si...]
    reduce_scatter x1, waiting for transfers between devices: 44.3 us -> 0.01 us  [per_device(): lax.psum_scatter((part_query + part_key + part_value).astype(jnp.bfloat16...]
    all_gather x1, waiting for transfers between devices: 2.78 us -> 33.9 us  [per_device(): lax.all_gather(grad_state.astype(bf16), 'tensor', axis=0, tiled=True)]
    convert_element_type x7 -> x0, other arithmetic: 13.3 us -> none  [per_device(): query_total, key_total, value_total, out_total, gate_total, up_total, dow...]
  transfers between devices with their start and end apart: 15 -> 8, of which waited for: 15 -> 7; matrix products, arithmetic and copies ran while one was open for 12% -> 8% of each run, Pallas kernels for 0% -> 34%
where the time goes in v1:
time: 832 us; the launch traced here: 827 us
  waiting for transfers between devices  289 us (35%)
  Pallas kernels  285 us (34%)
  matrix products  124 us (15%)
  blocking collectives  41.7 us (5%)
  other arithmetic  35.1 us (4%)
  local copies, waits for them, and re-layouts  34.7 us (4%)
  between operations  17.5 us (2%)
    pallas_call x2, Pallas kernels, weight_sums(): pl.pallas_call(functools.partial(weight_kernel, dp_size, count, x_of), ou...  285 us
    reduce_scatter x1, waiting for transfers between devices, per_device(): lax.psum_scatter(jnp.dot(attended, w_out, preferred_element_type=float_si...  71.8 us
    reduce_scatter x1, waiting for transfers between devices, per_device(): lax.psum_scatter(part_gate + part_up, 'tensor', scatter_dimension=0, tile...  60.9 us
    reduce_scatter x1, waiting for transfers between devices, per_device(): lax.psum_scatter(jnp.dot(hidden, w_down, preferred_element_type=float_sin...  44.1 us
    psum x1, blocking collectives, per_device(): lax.psum((gain_attn_part, gain_mlp_part), ('dp', 'tensor'))  41.7 us
    all_gather x1, waiting for transfers between devices, per_device(): lax.all_gather(grad_state.astype(bf16), 'tensor', axis=0, tiled=True)  33.9 us
    all_gather x1, waiting for transfers between devices, per_device(): normed_all = lax.all_gather(normed, 'tensor', axis=0, tiled=True)  33.4 us
    all_gather x1, waiting for transfers between devices, per_device(): mlp_all = lax.all_gather(normed_mlp, 'tensor', axis=0, tiled=True)  31.4 us
  transfers between devices with their start and end apart: 8, of which 7 were waited for; matrix products, arithmetic and copies ran while one was open for 8% of the time, Pallas kernels for 34%

profile of v1, /device:TPU:0, one launch (start us, length us, event | category | flops | bytes accessed | tf_op | source)
XLA Modules:
  0.0 827.4 jit_solution(13771581513095099996)
XLA Ops:
  15.4 33.4 %all-gather.5.cloned.1.call-done.refs_1_ = bf16[1024,2048]{1,0:T(8,128)(2,1)} async-done(((bf16[256,2048]{1,0:T(8,128)(2,1)}), bf16[1024,2048]{1,0:T(8,128)(2,1)}) %all-gather.5.cloned.1.call-update) | async-done | bytes 4194320 | tf_op jit(solution)/shard_map/all_gather | solution.py:183
  48.8 3.7 convolution_convert_fusion.4
  54.0 3.1 fusion.7
  57.1 6.2 fusion.2
  64.9 3.0 copy.126
  67.9 5.4 convolution_convert_fusion.2
  78.1 4.7 fusion.41
  87.6 5.6 fusion.42
  93.3 71.8 %reduce-scatter.5.cloned.1.call-done = f32[256,2048]{1,0:T(8,128)} async-done(((f32[1024,2048]{1,0:T(8,128)}), f32[256,2048]{1,0:T(8,128)}) %reduce-scatter.5.cloned.1.call-update) | async-done | bytes 2097168 | tf_op jit(solution)/shard_map/reduce_scatter | solution.py:238
  172.8 31.4 %all-gather.7.cloned.1.call-done.refs_1_ = bf16[1024,2048]{1,0:T(8,128)(2,1)} async-done(((bf16[256,2048]{1,0:T(8,128)(2,1)}), bf16[1024,2048]{1,0:T(8,128)(2,1)}) %all-gather.7.cloned.1.call-update) | async-done | bytes 4194320 | tf_op jit(solution)/shard_map/all_gather | solution.py:246
  204.2 12.4 %fusion.43 = f32[1024,1376]{1,0:T(8,128)} fusion(bf16[1024,2048]{1,0:T(8,128)(2,1)} %all-gather.7.cloned.1.call-done.refs_1_, bf16[2048,1376]{0,1:T(8,128)(2,1)} %param.31), kind=kOutput, calls=%fused_computation.93 | convolution fusion | flops 5771362304 | bytes 15466496 | tf_op jit(solution)/shard_map/dot_general | solution.py:247
  216.6 10.5 %fusion.44 = f32[1024,1376]{1,0:T(8,128)} fusion(bf16[1024,2048]{1,0:T(8,128)(2,1)S(1)} %copy-done.15, bf16[2048,1376]{0,1:T(8,128)(2,1)} %param.32), kind=kOutput, calls=%fused_computation.94 | convolution fusion | flops 5771362304 | bytes 15466496 | tf_op jit(solution)/shard_map/dot_general | solution.py:248
  227.1 13.2 %all-gather.9.cloned.1.call-done.refs_0_ = bf16[1024,2048]{1,0:T(8,128)(2,1)} async-done(((bf16[256,2048]{1,0:T(8,128)(2,1)}), bf16[1024,2048]{1,0:T(8,128)(2,1)}) %all-gather.9.cloned.1.call-update) | async-done | bytes 4194320 | tf_op jit(solution)/shard_map/all_gather | solution.py:260
  240.2 15.6 %multiply_convert_fusion.1 = (bf16[1024,1376]{1,0:T(8,128)(2,1)S(1)}, bf16[1024,1376]{1,0:T(8,128)(2,1)S(1)}, bf16[1024,1376]{1,0:T(8,128)(2,1)}) fusion(f32[1024,1376]{1,0:T(8,128)} %fusion.43, f32[1024,1376]{1,0:T(8,128)} %fusion.44, bf16[1024,2048]{1,0:T(8,128)(2,1)} %all-gather.9.cloned.1.call-done.refs_0_, bf16[1376,2048]{1,0:T(8,128)(2,1)} %param.33), kind=kOutput, calls=%fused_computation.3 | convolution fusion | flops 5792497664 | bytes 29556736 | tf_op jit(solution)/shard_map/td,fd->tf/dot_general | solution.py:261
  255.8 10.8 %fusion.45 = f32[1024,2048]{1,0:T(8,128)S(1)} fusion(bf16[1024,1376]{1,0:T(8,128)(2,1)S(1)} %get-tuple-element.134.refs_3_, bf16[2048,1376]{0,1:T(8,128)(2,1)} %param.31), kind=kOutput, calls=%fused_computation.95 | convolution fusion | flops 5771362304 | bytes 16842752 | tf_op jit(solution)/shard_map/tf,df->td/dot_general | solution.py:266
  266.6 10.9 %convolution_add_fusion = f32[1024,2048]{1,0:T(8,128)} fusion(f32[1024,2048]{1,0:T(8,128)S(1)} %fusion.45, bf16[1024,1376]{1,0:T(8,128)(2,1)S(1)} %get-tuple-element.133.refs_4_, bf16[2048,1376]{0,1:T(8,128)(2,1)} %param.32), kind=kOutput, calls=%fused_computation.12 | convolution fusion | flops 5773459456 | bytes 25231360 | tf_op jit(solution)/shard_map/tf,df->td/dot_general | solution.py:267
  277.6 10.9 %convolution_convert_fusion = bf16[1024,2048]{1,0:T(8,128)(2,1)} fusion(bf16[1024,1376]{1,0:T(8,128)(2,1)} %get-tuple-element.135.refs_2_, bf16[1376,2048]{1,0:T(8,128)(2,1)} %param.33), kind=kOutput, calls=%fused_computation.13 | convolution fusion | flops 5773459456 | bytes 12648448 | tf_op jit(solution)/shard_map/dot_general | solution.py:253
  288.6 60.9 %reduce-scatter.9.cloned.1.call-done = f32[256,2048]{1,0:T(8,128)} async-done(((f32[1024,2048]{1,0:T(8,128)}), f32[256,2048]{1,0:T(8,128)}) %reduce-scatter.9.cloned.1.call-update) | async-done | bytes 2097168 | tf_op jit(solution)/shard_map/reduce_scatter | solution.py:268
  349.5 2.8 multiply_reduce_fusion
  352.3 44.1 %reduce-scatter.7.cloned.1.call-done = bf16[256,2048]{1,0:T(8,128)(2,1)} async-done(((bf16[1024,2048]{1,0:T(8,128)(2,1)}), bf16[256,2048]{1,0:T(8,128)(2,1)}) %reduce-scatter.7.cloned.1.call-update) | async-done | bytes 1048592 | tf_op jit(solution)/shard_map/reduce_scatter | solution.py:252
  396.4 5.7 fusion.38
  402.8 33.9 %all-gather.11.cloned.1.call-done.refs_0_ = bf16[1024,2048]{1,0:T(8,128)(2,1)} async-done(((bf16[256,2048]{1,0:T(8,128)(2,1)}), bf16[1024,2048]{1,0:T(8,128)(2,1)}) %all-gather.11.cloned.1.call-update) | async-done | bytes 4194320 | tf_op jit(solution)/shard_map/all_gather | solution.py:273
  436.8 5.3 fusion.13
  458.5 3.2 add_convert_fusion
  463.7 218.7 %weight_sums.3 = (f32[256,1376]{1,0:T(8,128)}, f32[256,1376]{1,0:T(8,128)}, f32[256,1376]{1,0:T(8,128)}) custom-call(bf16[1024,2048]{1,0:T(8,128)(2,1)} %all-gather.9.cloned.1.call-done.refs_0_, bf16[1024,2048]{1,0:T(8,128)(2,1)} %all-gather.7.cloned.1.call-done.refs_1_, bf16[1024,1376]{1,0:T(8,128)(2,1)} %get-tuple-element.135.refs_2_, ...), custom_call_target="tpu_custom_call" | custom-call | tf_op jit(solution)/shard_map/weight_sums/pallas_call | solution.py:129
  682.4 2.9 copy.109
  685.3 2.9 copy.110
  688.2 2.9 copy.111
  695.0 2.6 pad_maximum_fusion.refs_3_
  697.7 66.7 %weight_sums.2 = (f32[256,512]{1,0:T(8,128)}, f32[256,640]{1,0:T(8,128)}) custom-call(bf16[1024,2048]{1,0:T(8,128)(2,1)} %all-gather.11.cloned.1.call-done.refs_0_, bf16[1024,2048]{1,0:T(8,128)(2,1)} %all-gather.5.cloned.1.call-done.refs_1_, bf16[1024,512]{1,0:T(8,128)(2,1)} %copy-done.16, bf16[1024,640]{1,0:T(8,128)(2,1)} %pad_maximum_fusion.refs_3_), custom_call_target="tpu_custom_call" | custom-call | tf_op jit(solution)/shard_map/weight_sums/pallas_call | solution.py:129
  772.9 41.7 %all-reduce.2 = (f32[2048]{0:T(1024)}, f32[2048]{0:T(1024)}, f32[]{:T(128)}) all-reduce(f32[2048]{0:T(1024)S(1)} %get-tuple-element.124, f32[2048]{0:T(1024)S(1)} %get-tuple-element.122, f32[]{:T(128)} %get-tuple-element.143), channel_id=1, replica_groups=mesh['dp'=8,'tensor'=4] {'dp','tensor'}, use_global_device_ids=true, to_apply=%region_12.0 | all-reduce | flops 4097 | bytes 32776 | tf_op jit(solution)/shard_map/psum | solution.py:353
  815.3 3.8 fusion.11
  (140 shorter events, 59.3 us)
Async XLA Ops:
  7.2 80.4 %copy-start = (bf16[512,2048]{1,0:T(8,128)(2,1)S(1)}, bf16[512,2048]{1,0:T(8,128)(2,1)}, u32[]{:S(2)}) copy-start(bf16[512,2048]{1,0:T(8,128)(2,1)} %param.30) | copy-start | bytes 6291460
  7.2 4.4 copy-start.30
  7.2 41.6 %copy-start.21 = (bf16[2048,64]{0,1:T(8,128)(2,1)S(1)}, bf16[2048,64]{0,1:T(8,128)(2,1)}, u32[]{:S(2)}) copy-start(bf16[2048,64]{0,1:T(8,128)(2,1)} %param.27) | copy-start | bytes 786436
  7.2 41.6 %all-gather.5.cloned.1.call-start = ((), (), s32[]{:S(2)}) async-start(), calls=%async_computation.4 | async-start | bytes 5242880 | tf_op jit(solution)/shard_map/all_gather | solution.py:183
  8.9 3.9 copy-start.27
  11.5 153.6 %reduce-scatter.5.cloned.1.call-start = ((), (), s32[]{:S(2)}) async-start(), calls=%async_computation.5 | async-start | bytes 10485760 | tf_op jit(solution)/shard_map/reduce_scatter | solution.py:238
  13.7 40.3 %copy-start.12 = (f32[512,512]{0,1:T(8,128)}, f32[512,512]{0,1:T(8,128)S(1)}, u32[]{:S(2)}) copy-start(f32[512,512]{0,1:T(8,128)S(1)} %and_convert_fusion) | copy-start | bytes 3145732
  48.8 3.8 copy-start.1
  48.8 3.8 copy-start.23
  54.0 3.2 copy-start.5
  67.9 5.4 copy-start.10
  67.9 5.5 copy-start.13
  73.3 4.8 copy-start.8
  93.2 71.9 %copy-start.4 = (bf16[256,2048]{1,0:T(8,128)(2,1)S(1)}, bf16[256,2048]{1,0:T(8,128)(2,1)}, u32[]{:S(2)}) copy-start(bf16[256,2048]{1,0:T(8,128)(2,1)} %param.24) | copy-start | bytes 3145732
  93.2 75.1 %copy-start.26 = (f32[2048]{0:T(1024)S(1)}, f32[2048]{0:T(1024)}, u32[]{:S(2)}) copy-start(f32[2048]{0:T(1024)} %param.26) | copy-start | bytes 24580
  93.2 111.0 %all-gather.7.cloned.1.call-start = ((), (), s32[]{:S(2)}) async-start(), calls=%async_computation.6 | async-start | bytes 5242880 | tf_op jit(solution)/shard_map/all_gather | solution.py:246
  169.6 70.7 %all-gather.9.cloned.1.call-start = ((), (), s32[]{:S(2)}) async-start(), calls=%async_computation.8 | async-start | bytes 5242880 | tf_op jit(solution)/shard_map/all_gather | solution.py:260
  172.8 176.7 %reduce-scatter.9.cloned.1.call-start = ((), (), s32[]{:S(2)}) async-start(), calls=%async_computation.9 | async-start | bytes 10485760 | tf_op jit(solution)/shard_map/reduce_scatter | solution.py:268
  204.2 12.4 %copy-start.15 = (bf16[1024,2048]{1,0:T(8,128)(2,1)S(1)}, bf16[1024,2048]{1,0:T(8,128)(2,1)}, u32[]{:S(2)}) copy-start(bf16[1024,2048]{1,0:T(8,128)(2,1)} %all-gather.7.cloned.1.call-done.refs_1_) | copy-start | bytes 12582916
  255.8 10.8 %copy-start.18 = (bf16[1024,1376]{1,0:T(8,128)(2,1)}, bf16[1024,1376]{1,0:T(8,128)(2,1)S(1)}, u32[]{:S(2)}) copy-start(bf16[1024,1376]{1,0:T(8,128)(2,1)S(1)} %get-tuple-element.134.refs_3_) | copy-start | bytes 8454148
  255.8 10.8 %copy-start.17 = (bf16[1024,1376]{1,0:T(8,128)(2,1)}, bf16[1024,1376]{1,0:T(8,128)(2,1)S(1)}, u32[]{:S(2)}) copy-start(bf16[1024,1376]{1,0:T(8,128)(2,1)S(1)} %get-tuple-element.133.refs_4_) | copy-start | bytes 8454148
  277.6 118.8 %reduce-scatter.7.cloned.1.call-start = ((), (), s32[]{:S(2)}) async-start(), calls=%async_computation.7 | async-start | bytes 5242880 | tf_op jit(solution)/shard_map/reduce_scatter | solution.py:252
  288.5 148.3 %all-gather.11.cloned.1.call-start = ((), (), s32[]{:S(2)}) async-start(), calls=%async_computation.10 | async-start | bytes 5242880 | tf_op jit(solution)/shard_map/all_gather | solution.py:273
  402.1 368.6 %reduce-scatter.11.cloned.1.call-start = ((), (), s32[]{:S(2)}) async-start(), calls=%async_computation.11 | async-start | bytes 5242880 | tf_op jit(solution)/shard_map/reduce_scatter | solution.py:331
  436.8 6.2 copy-start.11
  436.8 6.2 copy-start.14
  436.8 6.3 copy-start.20
  443.0 3.3 slice-start
  444.1 2.6 slice-start.1
  456.1 2.4 copy-start.24
  697.7 73.1 %copy-start.25 = (f32[2048]{0:T(1024)S(1)}, f32[2048]{0:T(1024)}, u32[]{:S(2)}) copy-start(f32[2048]{0:T(1024)} %param.25) | copy-start | bytes 24580
  697.7 73.1 %copy-start.28 = (f32[256]{0:T(256)S(1)}, f32[256]{0:T(256)}, u32[]{:S(2)}) copy-start(f32[256]{0:T(256)} %copy-done.27) | copy-start | bytes 3076
  (10 other events, 16.0 us)
Sparse Core Ops, SparseCore 0:
  11.6 37.1 all-gather.4
  93.3 71.7 reduce-scatter.4
  169.7 34.4 all-gather.6
  205.7 34.4 all-gather.8
  277.7 71.6 reduce-scatter.8
  351.8 44.5 reduce-scatter.6
  402.3 34.4 all-gather.10
  461.9 44.4 reduce-scatter.10
